TPU v7x, 32 devices: a whole 2x2x4 slice. The times are simulated.
32 devices in a mesh: user: 4 (over y, core), item: 8 (over z, x).
Axes of the slice: x: 2, y: 2, z: 4, core: 2. Of those that a mesh axis runs over, the one named last changes fastest.
Arguments:
- users: bfloat16 [4096, 256], P('user'), may hold values from -40 to 40
- catalog_vectors: bfloat16 [65536, 256], P('item'), may hold values from -8 to 8
- positives: int32 [4096], P('user'), may hold values from 0 to 65535
Outputs:
- loss: float32 [4096], P('user')
- user_grad: bfloat16 [4096, 256], P('user')
- item_grad: bfloat16 [65536, 256], P(('item', 'user'))
All inputs are finite; a program needn't handle non-finite values.
Results may differ from a plain program's by a relative error of at most 0.0034.
Values may be sent and summed in bfloat16 or wider, within the bound.
A program may use at most 64 MiB of HBM per device.

v0:
```python
import math

import jax
import jax.numpy as jnp
from jax import lax
from jax.sharding import PartitionSpec as P

sharpness_divisor = 4.0


def per_device(users, catalog_vectors, positives):
    rows = users.shape[0]
    count = catalog_vectors.shape[0]
    width = catalog_vectors.shape[1]
    block = math.gcd(count, 2048)
    nblock = count // block
    offset = lax.axis_index("item") * count
    local_pos = positives - offset
    stacked = catalog_vectors.reshape(nblock, block, width)
    numbers = jnp.arange(nblock, dtype=jnp.int32)
    columns = lax.broadcasted_iota(jnp.int32, (rows, block), 1)

    def scores_of(piece, number):
        raw_affinity_scores = lax.dot_general(
            users, piece, (((1,), (1,)), ((), ())), preferred_element_type=jnp.float32
        )
        positive_indicator = columns + number * block == local_pos[:, None]
        return (raw_affinity_scores / sharpness_divisor, positive_indicator)

    def first_pass(carry, inputs):
        piece, number = inputs
        run_max, run_sum, run_pos = carry
        affinity_grid, positive_indicator = scores_of(piece, number)
        new_max = jnp.maximum(run_max, jnp.max(affinity_grid, axis=1))
        run_sum = run_sum * jnp.exp(run_max - new_max) + jnp.sum(
            jnp.exp(affinity_grid - new_max[:, None]), axis=1
        )
        run_pos = run_pos + jnp.sum(jnp.where(positive_indicator, affinity_grid, 0.0), axis=1)
        return ((new_max, run_sum, run_pos), None)

    start = (
        jnp.full((rows,), -jnp.inf, jnp.float32),
        jnp.zeros((rows,), jnp.float32),
        jnp.zeros((rows,), jnp.float32),
    )
    (local_max, local_sum, local_hit), _ = lax.scan(first_pass, start, (stacked, numbers))
    global_max = lax.pmax(local_max, "item")
    global_sum, global_hit = lax.psum(
        (local_sum * jnp.exp(local_max - global_max), local_hit), "item"
    )
    lse = global_max + jnp.log(global_sum)
    loss = lse - global_hit

    def second_pass(accumulated_sum, inputs):
        piece, number = inputs
        affinity_grid, positive_indicator = scores_of(piece, number)
        normalized_probabilities = (
            jnp.exp(affinity_grid - lse[:, None]) - positive_indicator.astype(jnp.float32)
        ).astype(jnp.bfloat16)
        accumulated_sum = accumulated_sum + jnp.dot(
            normalized_probabilities, piece, preferred_element_type=jnp.float32
        )
        item_part = (
            lax.dot_general(
                normalized_probabilities,
                users,
                (((0,), (0,)), ((), ())),
                preferred_element_type=jnp.float32,
            )
            / sharpness_divisor
        )
        return (accumulated_sum, item_part)

    accumulated_sum, item_parts = lax.scan(
        second_pass, jnp.zeros((rows, width), jnp.float32), (stacked, numbers)
    )
    item_grad = lax.psum_scatter(
        item_parts.reshape(count, width), "user", scatter_dimension=0, tiled=True
    ).astype(jnp.bfloat16)
    customer_cost_addend = accumulated_sum / sharpness_divisor
    user_grad = lax.psum(customer_cost_addend, "item").astype(jnp.bfloat16)
    return (loss, user_grad, item_grad)


def solution(mesh):
    in_specs = (P("user", None), P("item", None), P("user"))
    out_specs = (P("user"), P("user", None), P(("item", "user"), None))
    return jax.shard_map(
        per_device, mesh=mesh, in_specs=in_specs, out_specs=out_specs, check_vma=False
    )
```

profile of v0, /device:TPU:27, one launch (start us, length us, event | category | flops | bytes accessed | tf_op | source)
XLA Modules:
  0.0 228.9 jit_solution(2953372545017226603)
XLA Ops:
  7.2 0.0 reduce-scatter.2.cloned.1.call-start
  7.3 0.7 broadcast_subtract_fusion
  8.0 47.3 %while.28 = (s32[]{:T(128)}, f32[1024]{0:T(1024)S(1)}, f32[1024]{0:T(1024)S(1)}, f32[1024]{0:T(1024)S(1)}, bf16[4,2048,256]{2,1,0:T(8,128)(2,1)}, /*index=5*/bf1...) while((s32[]{:T(128)}, f32[1024]{0:T(1024)S(1)}, ...), condition=%wide.region_4.5_spmd.clone, body=%wide.region_0.4_spmd.clone.sunk | while | flops 1092622336 | bytes 18424468 | solution.py:46
  8.0 5.9 %multiply_reduce_fusion.2 = (f32[1024]{0:T(1024)S(1)}, f32[2048,1024]{1,0:T(8,128)}) fusion(bf16[1024,256]{1,0:T(8,128)(2,1)} %get-tuple-element.340, bf16[4,2048,256]{2,1,0:T(8,128)(2,1)} %get-tuple-element.339, s32[]{:T(128)} %get-tuple-element.324), kind=kOutput, calls=%fused_computation.9.clone.1 | convolution fusion | flops 1077935104 | bytes 9966080 | tf_op jit(solution)/shard_map/while/body/eval_jaxpr/dot_general | solution.py:24
  13.8 0.6 dynamic_slice.38
  15.1 4.7 %fusion.39 = (f32[1024]{0:T(1024)S(1)}, f32[1024]{0:T(1024)S(1)}) fusion(f32[2048,1024]{1,0:T(8,128)} %get-tuple-element.300, s32[1024]{0:T(1024)S(1)} %get-tuple-element.342, s32[]{:T(128)} %bitcast.52, f32[1024]{0:T(1024)S(1)} %select_maximum_fusion.2), kind=kLoop, calls=%fused_computation.6.clone.1 | loop fusion | flops 14678016 | bytes 8404996 | tf_op jit(solution)/shard_map/while/body/eval_jaxpr/reduce_sum | solution.py:38
  19.8 5.9 %multiply_reduce_fusion.2 = (f32[1024]{0:T(1024)S(1)}, f32[2048,1024]{1,0:T(8,128)}) fusion(bf16[1024,256]{1,0:T(8,128)(2,1)} %get-tuple-element.340, bf16[4,2048,256]{2,1,0:T(8,128)(2,1)} %get-tuple-element.339, s32[]{:T(128)} %get-tuple-element.324), kind=kOutput, calls=%fused_computation.9.clone.1 | convolution fusion | flops 1077935104 | bytes 9966080 | tf_op jit(solution)/shard_map/while/body/eval_jaxpr/dot_general | solution.py:24
  25.7 0.6 dynamic_slice.38
  26.9 4.7 %fusion.39 = (f32[1024]{0:T(1024)S(1)}, f32[1024]{0:T(1024)S(1)}) fusion(f32[2048,1024]{1,0:T(8,128)} %get-tuple-element.300, s32[1024]{0:T(1024)S(1)} %get-tuple-element.342, s32[]{:T(128)} %bitcast.52, f32[1024]{0:T(1024)S(1)} %select_maximum_fusion.2), kind=kLoop, calls=%fused_computation.6.clone.1 | loop fusion | flops 14678016 | bytes 8404996 | tf_op jit(solution)/shard_map/while/body/eval_jaxpr/reduce_sum | solution.py:38
  31.6 5.9 %multiply_reduce_fusion.2 = (f32[1024]{0:T(1024)S(1)}, f32[2048,1024]{1,0:T(8,128)}) fusion(bf16[1024,256]{1,0:T(8,128)(2,1)} %get-tuple-element.340, bf16[4,2048,256]{2,1,0:T(8,128)(2,1)} %get-tuple-element.339, s32[]{:T(128)} %get-tuple-element.324), kind=kOutput, calls=%fused_computation.9.clone.1 | convolution fusion | flops 1077935104 | bytes 9966080 | tf_op jit(solution)/shard_map/while/body/eval_jaxpr/dot_general | solution.py:24
  37.5 0.6 dynamic_slice.38
  38.7 4.7 %fusion.39 = (f32[1024]{0:T(1024)S(1)}, f32[1024]{0:T(1024)S(1)}) fusion(f32[2048,1024]{1,0:T(8,128)} %get-tuple-element.300, s32[1024]{0:T(1024)S(1)} %get-tuple-element.342, s32[]{:T(128)} %bitcast.52, f32[1024]{0:T(1024)S(1)} %select_maximum_fusion.2), kind=kLoop, calls=%fused_computation.6.clone.1 | loop fusion | flops 14678016 | bytes 8404996 | tf_op jit(solution)/shard_map/while/body/eval_jaxpr/reduce_sum | solution.py:38
  43.5 5.9 %multiply_reduce_fusion.2 = (f32[1024]{0:T(1024)S(1)}, f32[2048,1024]{1,0:T(8,128)}) fusion(bf16[1024,256]{1,0:T(8,128)(2,1)} %get-tuple-element.340, bf16[4,2048,256]{2,1,0:T(8,128)(2,1)} %get-tuple-element.339, s32[]{:T(128)} %get-tuple-element.324), kind=kOutput, calls=%fused_computation.9.clone.1 | convolution fusion | flops 1077935104 | bytes 9966080 | tf_op jit(solution)/shard_map/while/body/eval_jaxpr/dot_general | solution.py:24
  49.3 0.6 dynamic_slice.38
  50.6 4.7 %fusion.39 = (f32[1024]{0:T(1024)S(1)}, f32[1024]{0:T(1024)S(1)}) fusion(f32[2048,1024]{1,0:T(8,128)} %get-tuple-element.300, s32[1024]{0:T(1024)S(1)} %get-tuple-element.342, s32[]{:T(128)} %bitcast.52, f32[1024]{0:T(1024)S(1)} %select_maximum_fusion.2), kind=kLoop, calls=%fused_computation.6.clone.1 | loop fusion | flops 14678016 | bytes 8404996 | tf_op jit(solution)/shard_map/while/body/eval_jaxpr/reduce_sum | solution.py:38
  55.3 13.4 %pmax.7 = f32[1024]{0:T(1024)S(1)} all-reduce(f32[1024]{0:T(1024)S(1)} %get-tuple-element.100), channel_id=1, replica_groups=mesh['user'=4,'item'=8] {'item'}, use_global_device_ids=true, to_apply=%region_5.6 | all-reduce | flops 1024 | bytes 8192 | tf_op jit(solution)/shard_map/pmax | solution.py:47
  68.7 15.3 %psum.21 = f32[1024]{0:T(1024)S(1)} all-reduce(f32[1024]{0:T(1024)S(1)} %exponential_multiply_fusion), channel_id=1, replica_groups=mesh['user'=4,'item'=8] {'item'}, use_global_device_ids=true, to_apply=%region_6.7 | all-reduce | flops 1024 | bytes 8192 | tf_op jit(solution)/shard_map/psum | solution.py:48
  84.1 54.9 %while.29 = (s32[]{:T(128)}, f32[1024,256]{1,0:T(8,128)S(1)}, f32[4,2048,256]{2,1,0:T(8,128)}, bf16[4,2048,256]{2,1,0:T(8,128)(2,1)}, bf16[1024,256]{1,0:T(8,128...) while((s32[]{:T(128)}, f32[1024,256]{1,0:T(8,128)S(1)}, ...), condition=%wide.region_9.10_spmd.clone, body=%wide.region_8.9_spmd.clone.sunk | while | flops 3236954112 | bytes 38807748 | solution.py:74
  84.1 0.6 dynamic_slice.41
  85.3 0.0 copy-start
  85.3 3.7 %fusion.46 = bf16[1024,2048]{0,1:T(8,128)(2,1)S(1)} fusion(bf16[1024,256]{1,0:T(8,128)(2,1)} %get-tuple-element.372, s32[1024]{0:T(1024)S(1)} %get-tuple-element.375, s32[]{:T(128)} %bitcast.61, f32[1024]{0:T(1024)S(1)} %get-tuple-element.373, bf16[4,2048,256]{2,1,0:T(8,128)(2,1)} %get-tuple-element.371, s32[]{:T(128)} %get-tuple-element.357), kind=kOutput, calls=%fused_computation.19.clone.1 | convolution fusion | flops 1088421888 | bytes 5776384 | tf_op jit(solution)/shard_map/while/body/eval_jaxpr/dot_general | solution.py:24
  89.1 0.0 copy-start.1
  89.1 2.0 copy-done.1
  91.1 0.0 copy-done
  91.1 2.6 %fusion.47 = f32[4,2048,256]{2,1,0:T(8,128)} fusion(f32[4,2048,256]{2,1,0:T(8,128)} %get-tuple-element.359, s32[]{:T(128)} %get-tuple-element.357, bf16[1024,2048]{0,1:T(8,128)(2,1)S(1)} %fusion.46, bf16[1024,256]{1,0:T(8,128)(2,1)S(1)} %copy-done), kind=kOutput, calls=%fused_computation.24.clone.1 | convolution fusion | flops 1074266112 | bytes 6816256 | tf_op jit(solution)/shard_map/while/body/eval_jaxpr/dot_general | solution.py:64
  93.7 4.1 %convolution_add_fusion.2 = f32[1024,256]{1,0:T(8,128)S(1)} fusion(bf16[1024,2048]{0,1:T(8,128)(2,1)} %copy-done.1, f32[1024,256]{1,0:T(8,128)S(1)} %get-tuple-element.358, bf16[4,2048,256]{2,1,0:T(8,128)(2,1)} %get-tuple-element.371, s32[]{:T(128)} %get-tuple-element.357, pred[]{:T(512)S(6)} %compare.7), kind=kOutput, calls=%fused_computation.25.clone.1 | convolution fusion | flops 1074266112 | bytes 7340545 | tf_op jit(solution)/shard_map/while/body/eval_jaxpr/dot_general | solution.py:60
  97.8 0.6 dynamic_slice.41
  99.1 0.0 copy-start
  99.1 3.7 %fusion.46 = bf16[1024,2048]{0,1:T(8,128)(2,1)S(1)} fusion(bf16[1024,256]{1,0:T(8,128)(2,1)} %get-tuple-element.372, s32[1024]{0:T(1024)S(1)} %get-tuple-element.375, s32[]{:T(128)} %bitcast.61, f32[1024]{0:T(1024)S(1)} %get-tuple-element.373, bf16[4,2048,256]{2,1,0:T(8,128)(2,1)} %get-tuple-element.371, s32[]{:T(128)} %get-tuple-element.357), kind=kOutput, calls=%fused_computation.19.clone.1 | convolution fusion | flops 1088421888 | bytes 5776384 | tf_op jit(solution)/shard_map/while/body/eval_jaxpr/dot_general | solution.py:24
  102.8 0.0 copy-start.1
  102.8 2.0 copy-done.1
  104.8 0.0 copy-done
  104.8 2.6 %fusion.47 = f32[4,2048,256]{2,1,0:T(8,128)} fusion(f32[4,2048,256]{2,1,0:T(8,128)} %get-tuple-element.359, s32[]{:T(128)} %get-tuple-element.357, bf16[1024,2048]{0,1:T(8,128)(2,1)S(1)} %fusion.46, bf16[1024,256]{1,0:T(8,128)(2,1)S(1)} %copy-done), kind=kOutput, calls=%fused_computation.24.clone.1 | convolution fusion | flops 1074266112 | bytes 6816256 | tf_op jit(solution)/shard_map/while/body/eval_jaxpr/dot_general | solution.py:64
  107.4 4.1 %convolution_add_fusion.2 = f32[1024,256]{1,0:T(8,128)S(1)} fusion(bf16[1024,2048]{0,1:T(8,128)(2,1)} %copy-done.1, f32[1024,256]{1,0:T(8,128)S(1)} %get-tuple-element.358, bf16[4,2048,256]{2,1,0:T(8,128)(2,1)} %get-tuple-element.371, s32[]{:T(128)} %get-tuple-element.357, pred[]{:T(512)S(6)} %compare.7), kind=kOutput, calls=%fused_computation.25.clone.1 | convolution fusion | flops 1074266112 | bytes 7340545 | tf_op jit(solution)/shard_map/while/body/eval_jaxpr/dot_general | solution.py:60
  111.5 0.6 dynamic_slice.41
  112.8 0.0 copy-start
  112.8 3.7 %fusion.46 = bf16[1024,2048]{0,1:T(8,128)(2,1)S(1)} fusion(bf16[1024,256]{1,0:T(8,128)(2,1)} %get-tuple-element.372, s32[1024]{0:T(1024)S(1)} %get-tuple-element.375, s32[]{:T(128)} %bitcast.61, f32[1024]{0:T(1024)S(1)} %get-tuple-element.373, bf16[4,2048,256]{2,1,0:T(8,128)(2,1)} %get-tuple-element.371, s32[]{:T(128)} %get-tuple-element.357), kind=kOutput, calls=%fused_computation.19.clone.1 | convolution fusion | flops 1088421888 | bytes 5776384 | tf_op jit(solution)/shard_map/while/body/eval_jaxpr/dot_general | solution.py:24
  116.5 0.0 copy-start.1
  116.5 2.0 copy-done.1
  118.5 0.0 copy-done
  118.5 2.6 %fusion.47 = f32[4,2048,256]{2,1,0:T(8,128)} fusion(f32[4,2048,256]{2,1,0:T(8,128)} %get-tuple-element.359, s32[]{:T(128)} %get-tuple-element.357, bf16[1024,2048]{0,1:T(8,128)(2,1)S(1)} %fusion.46, bf16[1024,256]{1,0:T(8,128)(2,1)S(1)} %copy-done), kind=kOutput, calls=%fused_computation.24.clone.1 | convolution fusion | flops 1074266112 | bytes 6816256 | tf_op jit(solution)/shard_map/while/body/eval_jaxpr/dot_general | solution.py:64
  121.1 4.1 %convolution_add_fusion.2 = f32[1024,256]{1,0:T(8,128)S(1)} fusion(bf16[1024,2048]{0,1:T(8,128)(2,1)} %copy-done.1, f32[1024,256]{1,0:T(8,128)S(1)} %get-tuple-element.358, bf16[4,2048,256]{2,1,0:T(8,128)(2,1)} %get-tuple-element.371, s32[]{:T(128)} %get-tuple-element.357, pred[]{:T(512)S(6)} %compare.7), kind=kOutput, calls=%fused_computation.25.clone.1 | convolution fusion | flops 1074266112 | bytes 7340545 | tf_op jit(solution)/shard_map/while/body/eval_jaxpr/dot_general | solution.py:60
  125.3 0.6 dynamic_slice.41
  126.5 0.0 copy-start
  126.5 3.7 %fusion.46 = bf16[1024,2048]{0,1:T(8,128)(2,1)S(1)} fusion(bf16[1024,256]{1,0:T(8,128)(2,1)} %get-tuple-element.372, s32[1024]{0:T(1024)S(1)} %get-tuple-element.375, s32[]{:T(128)} %bitcast.61, f32[1024]{0:T(1024)S(1)} %get-tuple-element.373, bf16[4,2048,256]{2,1,0:T(8,128)(2,1)} %get-tuple-element.371, s32[]{:T(128)} %get-tuple-element.357), kind=kOutput, calls=%fused_computation.19.clone.1 | convolution fusion | flops 1088421888 | bytes 5776384 | tf_op jit(solution)/shard_map/while/body/eval_jaxpr/dot_general | solution.py:24
  130.2 0.0 copy-start.1
  130.2 2.0 copy-done.1
  132.2 0.0 copy-done
  132.2 2.6 %fusion.47 = f32[4,2048,256]{2,1,0:T(8,128)} fusion(f32[4,2048,256]{2,1,0:T(8,128)} %get-tuple-element.359, s32[]{:T(128)} %get-tuple-element.357, bf16[1024,2048]{0,1:T(8,128)(2,1)S(1)} %fusion.46, bf16[1024,256]{1,0:T(8,128)(2,1)S(1)} %copy-done), kind=kOutput, calls=%fused_computation.24.clone.1 | convolution fusion | flops 1074266112 | bytes 6816256 | tf_op jit(solution)/shard_map/while/body/eval_jaxpr/dot_general | solution.py:64
  134.8 4.1 %convolution_add_fusion.2 = f32[1024,256]{1,0:T(8,128)S(1)} fusion(bf16[1024,2048]{0,1:T(8,128)(2,1)} %copy-done.1, f32[1024,256]{1,0:T(8,128)S(1)} %get-tuple-element.358, bf16[4,2048,256]{2,1,0:T(8,128)(2,1)} %get-tuple-element.371, s32[]{:T(128)} %get-tuple-element.357, pred[]{:T(512)S(6)} %compare.7), kind=kOutput, calls=%fused_computation.25.clone.1 | convolution fusion | flops 1074266112 | bytes 7340545 | tf_op jit(solution)/shard_map/while/body/eval_jaxpr/dot_general | solution.py:60
  139.0 0.0 reduce-scatter.2.cloned.1.call-update
  139.0 0.1 broadcast_multiply_fusion
  139.1 60.6 %all-reduce.2 = (f32[1024]{0:T(1024)S(1)}, bf16[1024,256]{1,0:T(8,128)(2,1)}) all-reduce(f32[1024]{0:T(1024)S(1)} %get-tuple-element.102, f32[1024,256]{1,0:T(8,128)S(1)} %broadcast_multiply_fusion), channel_id=1, replica_groups=mesh['user'=4,'item'=8] {'item'}, use_global_device_ids=true, to_apply=%region_7.8 | all-reduce | flops 263168 | bytes 1581056 | tf_op jit(solution)/shard_map/psum | solution.py:48
  199.7 0.6 sub.38
  200.3 19.1 %reduce-scatter.2.cloned.1.call-done = f32[2048,256]{1,0:T(8,128)} async-done(((f32[8192,256]{1,0:T(8,128)}), f32[2048,256]{1,0:T(8,128)}) %reduce-scatter.2.cloned.1.call-update) | async-done | bytes 2097168 | tf_op jit(solution)/shard_map/reduce_scatter | solution.py:77
  219.4 2.7 %convert_element_type.13 = bf16[2048,256]{1,0:T(8,128)(2,1)} convert(f32[2048,256]{1,0:T(8,128)} %reduce-scatter.2.cloned.1.call-done) | non-fusion elementwise | flops 524288 | bytes 3145728 | tf_op jit(solution)/shard_map/convert_element_type | solution.py:79
  (21 shorter events, 0.1 us)
Async XLA Ops:
  7.2 212.2 %reduce-scatter.2.cloned.1.call-start = ((), (), s32[]{:S(2)}) async-start(), calls=%async_computation.1 | async-start | bytes 10485760 | tf_op jit(solution)/shard_map/reduce_scatter | solution.py:77
  85.3 5.7 %copy-start = (bf16[1024,256]{1,0:T(8,128)(2,1)S(1)}, bf16[1024,256]{1,0:T(8,128)(2,1)}, u32[]{:S(2)}) copy-start(bf16[1024,256]{1,0:T(8,128)(2,1)} %get-tuple-element.372) | copy-start | bytes 1572868 | tf_op jit(solution)/shard_map/while
  89.1 2.0 copy-start.1
  99.1 5.7 %copy-start = (bf16[1024,256]{1,0:T(8,128)(2,1)S(1)}, bf16[1024,256]{1,0:T(8,128)(2,1)}, u32[]{:S(2)}) copy-start(bf16[1024,256]{1,0:T(8,128)(2,1)} %get-tuple-element.372) | copy-start | bytes 1572868 | tf_op jit(solution)/shard_map/while
  102.8 2.0 copy-start.1
  112.8 5.7 %copy-start = (bf16[1024,256]{1,0:T(8,128)(2,1)S(1)}, bf16[1024,256]{1,0:T(8,128)(2,1)}, u32[]{:S(2)}) copy-start(bf16[1024,256]{1,0:T(8,128)(2,1)} %get-tuple-element.372) | copy-start | bytes 1572868 | tf_op jit(solution)/shard_map/while
  116.5 2.0 copy-start.1
  126.5 5.7 %copy-start = (bf16[1024,256]{1,0:T(8,128)(2,1)S(1)}, bf16[1024,256]{1,0:T(8,128)(2,1)}, u32[]{:S(2)}) copy-start(bf16[1024,256]{1,0:T(8,128)(2,1)} %get-tuple-element.372) | copy-start | bytes 1572868 | tf_op jit(solution)/shard_map/while
  130.2 2.0 copy-start.1
Sparse Core Ops, SparseCore 0:
  139.1 80.2 reduce-scatter.1
where the time goes:
time: 233 us; the launch traced here: 229 us
  blocking collectives  89.3 us (38%)
  matrix products  65.3 us (28%)
  other arithmetic  22.9 us (10%)
  waiting for transfers between devices  19.1 us (8%)
  between operations  14.1 us (6%)
  local copies, waits for them, and re-layouts  12.6 us (5%)
  loops' own time  5.54 us (2%)
    psum x2, blocking collectives, per_device(): lax.psum((local_sum * jnp.exp(local_max - global_max), local_hit), 'item')  75.9 us
    dot_general x8, matrix products, scores_of(): lax.dot_general(users, piece, (((1,), (1,)), ((), ())), preferred_element...  38.3 us
    reduce_scatter x1, waiting for transfers between devices, per_device(): lax.psum_scatter(item_parts.reshape(count, width), 'user', scatter_dimens...  19.1 us
    reduce_sum x4, other arithmetic, first_pass(): jnp.sum(jnp.where(positive_indicator, affinity_grid, 0.0), axis=1)  18.8 us
    dot_general x4, matrix products, second_pass(): jnp.dot(normalized_probabilities, piece, preferred_element_type=jnp.float32)  16.5 us
    pmax x1, blocking collectives, per_device(): global_max = lax.pmax(local_max, 'item')  13.4 us
    dot_general x4, matrix products, second_pass(): lax.dot_general(normalized_probabilities, users, (((0,), (0,)), ((), ()))...  10.4 us
    while x20, local copies, waits for them, and re-layouts  7.91 us
  transfers between devices with their start and end apart: 1, of which 1 were waited for; matrix products, arithmetic and copies ran while one was open for 0% of the time, Pallas kernels for 0%

commit v1 on v0

v1 whole, which is shorter than its diff:
```python
import functools
import math

import jax
import jax.numpy as jnp
from jax import lax
from jax.experimental import pallas as pl
from jax.experimental.pallas import tpu as pltpu
from jax.sharding import PartitionSpec as P

sharpness_divisor = 4.0
inverse = 1.0 / sharpness_divisor
to_log2 = math.log2(math.e) / sharpness_divisor
MESH = pl.DeviceIdType.MESH


def kernel(
    n_item, step, tile, lanes,
    users_ref, items_ref, pos_ref,
    loss_ref, user_out, item_out,
    grown, score_a, score_b, tops, top, total, hits, stat_out, stat_in, hit_out, hit_in, factor,
    weight_a, weight_b, own_part, core_out, core_in, y_out, y_in, kept, user_sum,
    part_out, part_in, done, stat_sems, hit_sems, core_sems, y_sems, part_sems, done_sems,
):
    rows, width = users_ref.shape
    count = items_ref.shape[0]
    nstep = count // step
    own = count // 4
    per_block = own // step
    piece = width // n_item
    u = lax.axis_index("user")
    me = lax.axis_index("item")
    core = lax.rem(u, 2)
    y = u // 2
    core_peer = {"user": 2 * y + 1 - core, "item": me}
    y_peer = {"user": 2 * (1 - y) + core, "item": me}

    def item_peer(d):
        return {"user": u, "item": lax.rem(me + d, n_item)}

    barrier = pltpu.get_barrier_semaphore()
    for peer in [core_peer, y_peer] + [item_peer(d) for d in range(1, n_item)]:
        pl.semaphore_signal(barrier, inc=1, device_id=peer, device_id_type=MESH)

    top[...] = jnp.full_like(top, -jnp.inf)
    total[...] = jnp.zeros_like(total)
    hits[...] = jnp.zeros_like(hits)
    user_sum[...] = jnp.zeros_like(user_sum)
    groups = tile // 8
    first_row = lax.broadcasted_iota(jnp.int32, (groups, 1, 1), 0) * 8
    sublane = lax.broadcasted_iota(jnp.int32, (8, lanes), 0)
    offset = me * count

    def score(number, out):
        piece_rows = items_ref[pl.ds(pl.multiple_of(number * step, step), step), :]
        out[...] = lax.dot_general(
            piece_rows, users_ref[...], (((1,), (1,)), ((), ())),
            preferred_element_type=jnp.float32,
        )

    def grow(number, source):
        for t in range(step // tile):
            start = pl.multiple_of(number * step + t * tile, tile)
            for k in range(rows // lanes):
                cols = slice(k * lanes, (k + 1) * lanes)
                s = source[t * tile:(t + 1) * tile, cols].reshape(groups, 8, lanes)
                old = top[:, cols]
                new = jnp.maximum(old, jnp.max(s, axis=0))
                e = jnp.exp2((s - new[None]) * to_log2)
                grown[pl.ds(start, tile), cols] = e.reshape(tile, lanes)
                top[:, cols] = new
                tops[number * (step // tile) + t, :, cols] = new
                total[:, cols] = total[:, cols] * jnp.exp2((old - new) * to_log2) + jnp.sum(e, axis=0)
                rel = pos_ref[:, cols] - (offset + start) - sublane
                hits[:, cols] += jnp.sum(jnp.where(rel[None] == first_row, s, 0.0), axis=0)

    score(0, score_a)

    @pl.loop(0, nstep // 2)
    def _(i):
        score(2 * i + 1, score_b)
        grow(2 * i, score_a)
        score(jnp.minimum(2 * i + 2, nstep - 1), score_a)
        grow(2 * i + 1, score_b)

    m8 = top[...]
    m1 = jnp.max(m8, axis=0, keepdims=True)
    l1 = jnp.sum(total[...] * jnp.exp2((m8 - m1) * to_log2), axis=0, keepdims=True)
    p1 = jnp.sum(hits[...], axis=0, keepdims=True)
    stat_out[0:1, :] = m1
    stat_out[1:2, :] = l1
    hit_out[...] = p1
    pl.semaphore_wait(barrier, n_item + 1)
    stat_copies, hit_copies = [], []
    for d in range(1, n_item):
        stat_copies.append(pltpu.make_async_remote_copy(
            src_ref=stat_out, dst_ref=stat_in.at[d - 1], send_sem=stat_sems.at[0, d - 1],
            recv_sem=stat_sems.at[1, d - 1], device_id=item_peer(d), device_id_type=MESH))
        stat_copies[-1].start()
    for d in range(1, n_item):
        hit_copies.append(pltpu.make_async_remote_copy(
            src_ref=hit_out, dst_ref=hit_in.at[d - 1], send_sem=hit_sems.at[0, d - 1],
            recv_sem=hit_sems.at[1, d - 1], device_id=item_peer(d), device_id_type=MESH))
        hit_copies[-1].start()
    for copy in stat_copies:
        copy.wait()
    all_top = m1
    for d in range(n_item - 1):
        all_top = jnp.maximum(all_top, stat_in[d, 0:1, :])
    all_sum = l1 * jnp.exp2((m1 - all_top) * to_log2)
    for d in range(n_item - 1):
        all_sum = all_sum + stat_in[d, 1:2, :] * jnp.exp2((stat_in[d, 0:1, :] - all_top) * to_log2)
    loss_ref[...] = all_top * inverse + jnp.log(all_sum)
    factor[0:1, :] = all_top
    factor[1:2, :] = 1.0 / all_sum

    def weigh(start, out):
        for t in range(step // tile):
            begin = pl.multiple_of(start + t * tile, tile)
            for k in range(rows // lanes):
                cols = slice(k * lanes, (k + 1) * lanes)
                f = jnp.exp2((tops[begin // tile, :, cols] - factor[0:1, cols]) * to_log2) * factor[1:2, cols]
                w = grown[pl.ds(begin, tile), cols].reshape(groups, 8, lanes) * f[None]
                rel = pos_ref[:, cols] - (offset + begin) - sublane
                w = jnp.where(rel[None] == first_row, w - 1.0, w)
                out[t * tile:(t + 1) * tile, cols] = w.reshape(tile, lanes).astype(jnp.bfloat16)

    def item_part(weight):
        return jnp.dot(weight[...], users_ref[...], preferred_element_type=jnp.float32) * inverse

    def user_part(start, weight):
        return lax.dot_general(
            items_ref[pl.ds(start, step), :], weight[...], (((0,), (0,)), ((), ())),
            preferred_element_type=jnp.float32,
        )

    def core_copy(q):
        return pltpu.make_async_remote_copy(
            src_ref=core_out.at[q], dst_ref=core_in.at[q], send_sem=core_sems.at[0, q],
            recv_sem=core_sems.at[1, q], device_id=core_peer, device_id_type=MESH)

    def y_copy(q):
        return pltpu.make_async_remote_copy(
            src_ref=y_out.at[q], dst_ref=y_in.at[q], send_sem=y_sems.at[0, q],
            recv_sem=y_sems.at[1, q], device_id=y_peer, device_id_type=MESH)

    def settle(q):
        core_copy(q).wait_recv()
        both = own_part[q % 2] + core_in[q].astype(jnp.float32)

        @pl.when(q < per_block)
        def _():
            y_out[q % per_block] = both.astype(jnp.bfloat16)
            y_copy(q % per_block).start()

        @pl.when(q >= per_block)
        def _():
            kept[q % per_block] = both

    @pl.loop(0, 2 * per_block)
    def _(q):
        far = 1 - q // per_block
        block_y = lax.rem(y + far, 2)
        inner = lax.rem(q, per_block) * step
        start_a = pl.multiple_of((2 * block_y + 1 - core) * own + inner, step)
        start_b = pl.multiple_of((2 * block_y + core) * own + inner, step)
        weigh(start_a, weight_a)
        core_out[q] = item_part(weight_a).astype(jnp.bfloat16)
        weigh(start_b, weight_b)
        part_a = user_part(start_a, weight_a)
        core_copy(q).start()
        own_part[q % 2] = item_part(weight_b)
        user_sum[...] += part_a + user_part(start_b, weight_b)

        @pl.when(q >= 1)
        def _():
            settle(q - 1)

    part_out[...] = (user_sum[...] * inverse).astype(jnp.bfloat16).reshape(part_out.shape)
    part_copies = []
    for d in range(1, n_item):
        part_copies.append(pltpu.make_async_remote_copy(
            src_ref=part_out.at[lax.rem(me + d, n_item)], dst_ref=part_in.at[d - 1],
            send_sem=part_sems.at[0, d - 1], recv_sem=part_sems.at[1, d - 1],
            device_id=item_peer(d), device_id_type=MESH))
        part_copies[-1].start()
    settle(2 * per_block - 1)
    for copy in hit_copies:
        copy.wait()
    p_all = p1
    for d in range(n_item - 1):
        p_all = p_all + hit_in[d]
    loss_ref[...] = loss_ref[...] - p_all * inverse
    mine = user_sum[pl.ds(pl.multiple_of(me * piece, piece), piece), :] * inverse
    for d in range(n_item - 1):
        part_copies[d].wait()
        mine = mine + part_in[d].astype(jnp.float32)
    done[me] = mine.astype(jnp.bfloat16)
    done_copies = []
    for d in range(1, n_item):
        done_copies.append(pltpu.make_async_remote_copy(
            src_ref=done.at[me], dst_ref=done.at[me],
            send_sem=done_sems.at[0, d - 1], recv_sem=done_sems.at[1, d - 1],
            device_id=item_peer(d), device_id_type=MESH))
        done_copies[-1].start()
    for q in range(per_block):
        y_copy(q).wait()
        item_out[q * step:(q + 1) * step, :] = (kept[q] + y_in[q].astype(jnp.float32)).astype(jnp.bfloat16)
    for q in range(2 * per_block):
        core_copy(q).wait_send()
    for copy in done_copies:
        copy.wait()
    user_out[...] = done[...].reshape(user_out.shape)


def solution(mesh):
    n_item = mesh.shape["item"]
    assert mesh.shape["user"] == 4

    def per_device(users, catalog_vectors, positives):
        rows, width = users.shape
        count = catalog_vectors.shape[0]
        own = count // 4
        step, tile, lanes = min(512, own), 256, 128
        per_block = own // step
        piece = width // n_item
        f32, bf16 = jnp.float32, jnp.bfloat16
        vmem = pl.BlockSpec(memory_space=pltpu.VMEM)
        dma = pltpu.SemaphoreType.DMA
        loss, user_t, item_grad = pl.pallas_call(
            functools.partial(kernel, n_item, step, tile, lanes),
            out_shape=(
                jax.ShapeDtypeStruct((1, rows), f32),
                jax.ShapeDtypeStruct((width, rows), bf16),
                jax.ShapeDtypeStruct((own, width), bf16),
            ),
            in_specs=[vmem] * 3,
            out_specs=(vmem,) * 3,
            scratch_shapes=[
                pltpu.VMEM((count, rows), f32),
                pltpu.VMEM((step, rows), f32),
                pltpu.VMEM((step, rows), f32),
                pltpu.VMEM((count // tile, 8, rows), f32),
                pltpu.VMEM((8, rows), f32),
                pltpu.VMEM((8, rows), f32),
                pltpu.VMEM((8, rows), f32),
                pltpu.VMEM((2, rows), f32),
                pltpu.VMEM((n_item - 1, 2, rows), f32),
                pltpu.VMEM((1, rows), f32),
                pltpu.VMEM((n_item - 1, 1, rows), f32),
                pltpu.VMEM((2, rows), f32),
                pltpu.VMEM((step, rows), bf16),
                pltpu.VMEM((step, rows), bf16),
                pltpu.VMEM((2, step, width), f32),
                pltpu.VMEM((2 * per_block, step, width), bf16),
                pltpu.VMEM((2 * per_block, step, width), bf16),
                pltpu.VMEM((per_block, step, width), bf16),
                pltpu.VMEM((per_block, step, width), bf16),
                pltpu.VMEM((per_block, step, width), f32),
                pltpu.VMEM((width, rows), f32),
                pltpu.VMEM((n_item, piece, rows), bf16),
                pltpu.VMEM((n_item - 1, piece, rows), bf16),
                pltpu.VMEM((n_item, piece, rows), bf16),
                dma((2, n_item - 1)),
                dma((2, n_item - 1)),
                dma((2, 2 * per_block)),
                dma((2, per_block)),
                dma((2, n_item - 1)),
                dma((2, n_item - 1)),
            ],
            compiler_params=pltpu.CompilerParams(
                collective_id=0, has_side_effects=True, vmem_limit_bytes=63 * 1024 * 1024,
            ),
        )(users, catalog_vectors, positives.reshape(1, rows))
        return loss.reshape(rows), user_t.T, item_grad

    in_specs = (P("user", None), P("item", None), P("user"))
    out_specs = (P("user"), P("user", None), P(("item", "user"), None))
    return jax.shard_map(
        per_device, mesh=mesh, in_specs=in_specs, out_specs=out_specs, check_vma=False
    )
```

time: 233 us -> 77.5 us (0.33); the launches traced: 229 us -> 77.3 us
  blocking collectives: 89.3 us -> 0 us
  Pallas kernels: 0 us -> 71 us
  matrix products: 65.3 us -> 0 us
  other arithmetic: 22.9 us -> 0 us
  waiting for transfers between devices: 19.1 us -> 0 us
  between operations: 14.1 us -> 0.64 us
  local copies, waits for them, and re-layouts: 12.6 us -> 5.58 us
  loops' own time: 5.54 us -> 0 us
    psum x2 -> x0, blocking collectives: 75.9 us -> none  [per_device(): lax.psum((local_sum * jnp.exp(local_max - global_max), local_hit), 'item')]
    pallas_call x0 -> x1, Pallas kernels: none -> 71 us  [per_device(): pl.pallas_call(functools.partial(kernel, n_item, step, tile, lanes), out_...]
    dot_general x16 -> x0, matrix products: 65.3 us -> none  [the longest x8 38.3 us: scores_of(): lax.dot_general(users, piece, (((1,), (1,)), ((), ())), preferred_element...]
    reduce_scatter x1 -> x0, waiting for transfers between devices: 19.1 us -> none  [per_device(): lax.psum_scatter(item_parts.reshape(count, width), 'user', scatter_dimens...]
    reduce_sum x4 -> x0, other arithmetic: 18.8 us -> none  [first_pass(): jnp.sum(jnp.where(positive_indicator, affinity_grid, 0.0), axis=1)]
    pmax x1 -> x0, blocking collectives: 13.4 us -> none  [per_device(): global_max = lax.pmax(local_max, 'item')]
    while x20 -> x0, local copies, waits for them, and re-layouts: 7.91 us -> none
    unnamed x0 -> x3, local copies, waits for them, and re-layouts: none -> 5.58 us
  transfers between devices with their start and end apart: 1 -> 0, of which waited for: 1 -> 0; matrix products, arithmetic and copies ran while one was open for 0% -> 0% of each run, Pallas kernels for 0% -> 0%
where the time goes in v1:
time: 77.5 us; the launch traced here: 77.3 us
  Pallas kernels  71 us (92%)
  local copies, waits for them, and re-layouts  5.58 us (7%)
    pallas_call x1, Pallas kernels, per_device(): pl.pallas_call(functools.partial(kernel, n_item, step, tile, lanes), out_...  71 us
    unnamed x3, local copies, waits for them, and re-layouts  5.58 us

profile of v1, /device:TPU:27, one launch (start us, length us, event | category | flops | bytes accessed | tf_op | source)
XLA Modules:
  0.0 77.3 jit_solution(5101961932897979422)
XLA Ops:
  0.6 71.0 %shard_map.58 = (f32[1,1024]{1,0:T(1,128)}, bf16[256,1024]{1,0:T(8,128)(2,1)}, bf16[2048,256]{1,0:T(8,128)(2,1)}) custom-call(bf16[1024,256]{1,0:T(8,128)(2,1)} %users_ref.1, bf16[8192,256]{1,0:T(8,128)(2,1)} %items_ref.1, s32[1,1024]{1,0:T(1,128)} %bitcast.5), custom_call_target="tpu_custom_call" | custom-call | tf_op jit(solution)/shard_map/pallas_call | solution.py:230
  71.7 2.0 %copy.6 = bf16[1024,256]{1,0:T(8,128)(2,1)} copy(bf16[1024,256]{0,1:T(8,128)(2,1)} %bitcast.3) | data formatting | bytes 1048576
  73.7 1.3 %copy.9 = f32[1024]{0:T(1024)} copy(f32[1024]{0:T(1024)} %bitcast.4) | data formatting | bytes 8192
  75.0 2.3 %copy.10 = bf16[2048,256]{1,0:T(8,128)(2,1)} copy(bf16[2048,256]{1,0:T(8,128)(2,1)} %get-tuple-element.17) | data formatting | bytes 2097152

commit v2 on v1

--- a/solution.py
+++ b/solution.py
@@ -1,5 +1,4 @@
 import functools
-import math
 
 import jax
 import jax.numpy as jnp
@@ -10,7 +9,6 @@
 
 sharpness_divisor = 4.0
 inverse = 1.0 / sharpness_divisor
-to_log2 = math.log2(math.e) / sharpness_divisor
 MESH = pl.DeviceIdType.MESH
 
 
@@ -20,7 +18,7 @@
     loss_ref, user_out, item_out,
     grown, score_a, score_b, tops, top, total, hits, stat_out, stat_in, hit_out, hit_in, factor,
     weight_a, weight_b, own_part, core_out, core_in, y_out, y_in, kept, user_sum,
-    part_out, part_in, done, stat_sems, hit_sems, core_sems, y_sems, part_sems, done_sems,
+    part_out, part_in, done, quarter, stat_sems, hit_sems, core_sems, y_sems, part_sems, done_sems,
 ):
     rows, width = users_ref.shape
     count = items_ref.shape[0]
@@ -46,46 +44,58 @@
     total[...] = jnp.zeros_like(total)
     hits[...] = jnp.zeros_like(hits)
     user_sum[...] = jnp.zeros_like(user_sum)
+    quarter[...] = users_ref[...] * jnp.bfloat16(inverse)
     groups = tile // 8
     first_row = lax.broadcasted_iota(jnp.int32, (groups, 1, 1), 0) * 8
     sublane = lax.broadcasted_iota(jnp.int32, (8, lanes), 0)
     offset = me * count
 
-    def score(number, out):
+    wide = 2 * lanes
+    pieces = rows // wide
+
+    def score(number, out, k):
+        cols = slice(k * wide, (k + 1) * wide)
         piece_rows = items_ref[pl.ds(pl.multiple_of(number * step, step), step), :]
-        out[...] = lax.dot_general(
-            piece_rows, users_ref[...], (((1,), (1,)), ((), ())),
+        out[:, cols] = lax.dot_general(
+            piece_rows, quarter[cols, :], (((1,), (1,)), ((), ())),
             preferred_element_type=jnp.float32,
         )
 
-    def grow(number, source):
-        for t in range(step // tile):
-            start = pl.multiple_of(number * step + t * tile, tile)
-            for k in range(rows // lanes):
-                cols = slice(k * lanes, (k + 1) * lanes)
+    def grow(number, source, piece_number):
+        for k in (2 * piece_number, 2 * piece_number + 1):
+            cols = slice(k * lanes, (k + 1) * lanes)
+            old, run, hit = top[:, cols], total[:, cols], hits[:, cols]
+            for t in range(step // tile):
+                start = pl.multiple_of(number * step + t * tile, tile)
                 s = source[t * tile:(t + 1) * tile, cols].reshape(groups, 8, lanes)
-                old = top[:, cols]
                 new = jnp.maximum(old, jnp.max(s, axis=0))
-                e = jnp.exp2((s - new[None]) * to_log2)
+                e = jnp.exp(s - new[None])
                 grown[pl.ds(start, tile), cols] = e.reshape(tile, lanes)
-                top[:, cols] = new
                 tops[number * (step // tile) + t, :, cols] = new
-                total[:, cols] = total[:, cols] * jnp.exp2((old - new) * to_log2) + jnp.sum(e, axis=0)
+                run = run * jnp.exp(old - new) + jnp.sum(e, axis=0)
+                old = new
                 rel = pos_ref[:, cols] - (offset + start) - sublane
-                hits[:, cols] += jnp.sum(jnp.where(rel[None] == first_row, s, 0.0), axis=0)
-
-    score(0, score_a)
+                for g in range(groups):
+                    hit = jnp.where(rel == 8 * g, s[g], hit)
+            top[:, cols] = old
+            total[:, cols] = run
+            hits[:, cols] = hit
+
+    for k in range(pieces):
+        score(0, score_a, k)
 
     @pl.loop(0, nstep // 2)
     def _(i):
-        score(2 * i + 1, score_b)
-        grow(2 * i, score_a)
-        score(jnp.minimum(2 * i + 2, nstep - 1), score_a)
-        grow(2 * i + 1, score_b)
+        for k in range(pieces):
+            score(2 * i + 1, score_b, k)
+            grow(2 * i, score_a, k)
+        for k in range(pieces):
+            score(jnp.minimum(2 * i + 2, nstep - 1), score_a, k)
+            grow(2 * i + 1, score_b, k)
 
     m8 = top[...]
     m1 = jnp.max(m8, axis=0, keepdims=True)
-    l1 = jnp.sum(total[...] * jnp.exp2((m8 - m1) * to_log2), axis=0, keepdims=True)
+    l1 = jnp.sum(total[...] * jnp.exp(m8 - m1), axis=0, keepdims=True)
     p1 = jnp.sum(hits[...], axis=0, keepdims=True)
     stat_out[0:1, :] = m1
     stat_out[1:2, :] = l1
@@ -107,30 +117,33 @@
     all_top = m1
     for d in range(n_item - 1):
         all_top = jnp.maximum(all_top, stat_in[d, 0:1, :])
-    all_sum = l1 * jnp.exp2((m1 - all_top) * to_log2)
+    all_sum = l1 * jnp.exp(m1 - all_top)
     for d in range(n_item - 1):
-        all_sum = all_sum + stat_in[d, 1:2, :] * jnp.exp2((stat_in[d, 0:1, :] - all_top) * to_log2)
-    loss_ref[...] = all_top * inverse + jnp.log(all_sum)
+        all_sum = all_sum + stat_in[d, 1:2, :] * jnp.exp(stat_in[d, 0:1, :] - all_top)
+    loss_ref[...] = all_top + jnp.log(all_sum)
     factor[0:1, :] = all_top
     factor[1:2, :] = 1.0 / all_sum
 
-    def weigh(start, out):
-        for t in range(step // tile):
-            begin = pl.multiple_of(start + t * tile, tile)
-            for k in range(rows // lanes):
-                cols = slice(k * lanes, (k + 1) * lanes)
-                f = jnp.exp2((tops[begin // tile, :, cols] - factor[0:1, cols]) * to_log2) * factor[1:2, cols]
+    def weigh(start, out, piece_number):
+        for k in (2 * piece_number, 2 * piece_number + 1):
+            cols = slice(k * lanes, (k + 1) * lanes)
+            for t in range(step // tile):
+                begin = pl.multiple_of(start + t * tile, tile)
+                f = jnp.exp(tops[begin // tile, :, cols] - factor[0:1, cols]) * factor[1:2, cols]
                 w = grown[pl.ds(begin, tile), cols].reshape(groups, 8, lanes) * f[None]
                 rel = pos_ref[:, cols] - (offset + begin) - sublane
                 w = jnp.where(rel[None] == first_row, w - 1.0, w)
                 out[t * tile:(t + 1) * tile, cols] = w.reshape(tile, lanes).astype(jnp.bfloat16)
 
-    def item_part(weight):
-        return jnp.dot(weight[...], users_ref[...], preferred_element_type=jnp.float32) * inverse
-
-    def user_part(start, weight):
-        return lax.dot_general(
-            items_ref[pl.ds(start, step), :], weight[...], (((0,), (0,)), ((), ())),
+    def item_part(weight, t):
+        return jnp.dot(
+            weight[t * half:(t + 1) * half, :], users_ref[...], preferred_element_type=jnp.float32
+        ) * inverse
+
+    def user_part(start, weight, k):
+        cols = slice(k * wide, (k + 1) * wide)
+        user_sum[:, cols] += lax.dot_general(
+            items_ref[pl.ds(start, step), :], weight[:, cols], (((0,), (0,)), ((), ())),
             preferred_element_type=jnp.float32,
         )
 
@@ -157,20 +170,34 @@
         def _():
             kept[q % per_block] = both
 
-    @pl.loop(0, 2 * per_block)
-    def _(q):
+    def starts(q):
         far = 1 - q // per_block
         block_y = lax.rem(y + far, 2)
         inner = lax.rem(q, per_block) * step
         start_a = pl.multiple_of((2 * block_y + 1 - core) * own + inner, step)
         start_b = pl.multiple_of((2 * block_y + core) * own + inner, step)
-        weigh(start_a, weight_a)
-        core_out[q] = item_part(weight_a).astype(jnp.bfloat16)
-        weigh(start_b, weight_b)
-        part_a = user_part(start_a, weight_a)
+        return start_a, start_b
+
+    first = starts(0)[0]
+    for k in range(pieces):
+        weigh(first, weight_a, k)
+    halves, half = 2, step // 2
+
+    @pl.loop(0, 2 * per_block)
+    def _(q):
+        start_a, start_b = starts(q)
+        next_a = starts(jnp.minimum(q + 1, 2 * per_block - 1))[0]
+        for k in range(pieces):
+            if k < halves:
+                core_out[q, k * half:(k + 1) * half, :] = item_part(weight_a, k).astype(jnp.bfloat16)
+            weigh(start_b, weight_b, k)
+            user_part(start_a, weight_a, k)
         core_copy(q).start()
-        own_part[q % 2] = item_part(weight_b)
-        user_sum[...] += part_a + user_part(start_b, weight_b)
+        for k in range(pieces):
+            if k < halves:
+                own_part[q % 2, k * half:(k + 1) * half, :] = item_part(weight_b, k)
+            weigh(next_a, weight_a, k)
+            user_part(start_b, weight_b, k)
 
         @pl.when(q >= 1)
         def _():
@@ -190,7 +217,7 @@
     p_all = p1
     for d in range(n_item - 1):
         p_all = p_all + hit_in[d]
-    loss_ref[...] = loss_ref[...] - p_all * inverse
+    loss_ref[...] = loss_ref[...] - p_all
     mine = user_sum[pl.ds(pl.multiple_of(me * piece, piece), piece), :] * inverse
     for d in range(n_item - 1):
         part_copies[d].wait()
@@ -210,7 +237,13 @@
         core_copy(q).wait_send()
     for copy in done_copies:
         copy.wait()
-    user_out[...] = done[...].reshape(user_out.shape)
+    user_out[...] = done[...].reshape(width, rows).astype(jnp.float32).T.astype(jnp.bfloat16)
+
+
+def hand_on(a, b, c, x, y, z):
+    x[...] = a[...]
+    y[...] = b[...]
+    z[...] = c[...]
 
 
 def solution(mesh):
@@ -221,17 +254,17 @@
         rows, width = users.shape
         count = catalog_vectors.shape[0]
         own = count // 4
-        step, tile, lanes = min(512, own), 256, 128
+        step, tile, lanes = min(512, own), 128, 128
         per_block = own // step
         piece = width // n_item
         f32, bf16 = jnp.float32, jnp.bfloat16
         vmem = pl.BlockSpec(memory_space=pltpu.VMEM)
         dma = pltpu.SemaphoreType.DMA
-        loss, user_t, item_grad = pl.pallas_call(
+        results = pl.pallas_call(
             functools.partial(kernel, n_item, step, tile, lanes),
             out_shape=(
                 jax.ShapeDtypeStruct((1, rows), f32),
-                jax.ShapeDtypeStruct((width, rows), bf16),
+                jax.ShapeDtypeStruct((rows, width), bf16),
                 jax.ShapeDtypeStruct((own, width), bf16),
             ),
             in_specs=[vmem] * 3,
@@ -261,6 +294,7 @@
                 pltpu.VMEM((n_item, piece, rows), bf16),
                 pltpu.VMEM((n_item - 1, piece, rows), bf16),
                 pltpu.VMEM((n_item, piece, rows), bf16),
+                pltpu.VMEM((rows, width), bf16),
                 dma((2, n_item - 1)),
                 dma((2, n_item - 1)),
                 dma((2, 2 * per_block)),
@@ -272,7 +306,14 @@
                 collective_id=0, has_side_effects=True, vmem_limit_bytes=63 * 1024 * 1024,
             ),
         )(users, catalog_vectors, positives.reshape(1, rows))
-        return loss.reshape(rows), user_t.T, item_grad
+        loss, user_grad, item_grad = pl.pallas_call(
+            hand_on,
+            out_shape=tuple(jax.ShapeDtypeStruct(r.shape, r.dtype) for r in results),
+            in_specs=[vmem] * 3,
+            out_specs=(vmem,) * 3,
+            compiler_params=pltpu.CompilerParams(vmem_limit_bytes=8 * 1024 * 1024),
+        )(*results)
+        return loss.reshape(rows), user_grad, item_grad
 
     in_specs = (P("user", None), P("item", None), P("user"))
     out_specs = (P("user"), P("user", None), P(("item", "user"), None))

time: 77.5 us -> 74.7 us (0.964)
  local copies, waits for them, and re-layouts: 5.58 us -> 2.94 us
    unnamed x3 -> x6, local copies, waits for them, and re-layouts: 5.58 us -> 2.94 us
    pallas_call x1, Pallas kernels: 71 us -> 69.6 us  [per_device(): pl.pallas_call(functools.partial(kernel, n_item, step, tile, lanes), out_...]
    pallas_call x0 -> x1, Pallas kernels: none -> 1.24 us  [per_device(): pl.pallas_call(hand_on, out_shape=tuple((jax.ShapeDtypeStruct(r.shape, r....]
where the time goes in v2:
time: 74.7 us; the launch traced here: 74.4 us
  Pallas kernels  70.8 us (95%)
  local copies, waits for them, and re-layouts  2.94 us (4%)
    pallas_call x1, Pallas kernels, per_device(): pl.pallas_call(functools.partial(kernel, n_item, step, tile, lanes), out_...  69.6 us
    unnamed x6, local copies, waits for them, and re-layouts  2.94 us

profile of v2, /device:TPU:27, one launch (start us, length us, event | category | flops | bytes accessed | tf_op | source)
XLA Modules:
  0.0 74.4 jit_solution(16925455697594783750)
XLA Ops:
  0.6 69.6 %shard_map.58 = (f32[1,1024]{1,0:T(1,128)}, bf16[1024,256]{1,0:T(8,128)(2,1)}, bf16[2048,256]{1,0:T(8,128)(2,1)}) custom-call(bf16[1024,256]{1,0:T(8,128)(2,1)} %users_ref.1, bf16[8192,256]{1,0:T(8,128)(2,1)} %items_ref.1, s32[1,1024]{1,0:T(1,128)} %bitcast.2), custom_call_target="tpu_custom_call" | custom-call | tf_op jit(solution)/shard_map/pallas_call | solution.py:263
  70.2 0.0 copy-start
  70.2 1.2 %copy-done = bf16[2048,256]{1,0:T(8,128)(2,1)S(1)} copy-done((bf16[2048,256]{1,0:T(8,128)(2,1)S(1)}, bf16[2048,256]{1,0:T(8,128)(2,1)}, u32[]{:S(2)}) %copy-start) | copy-done | bytes 1048600
  71.5 0.0 copy-start.1
  71.5 1.0 %copy-done.1 = bf16[1024,256]{1,0:T(8,128)(2,1)S(1)} copy-done((bf16[1024,256]{1,0:T(8,128)(2,1)S(1)}, bf16[1024,256]{1,0:T(8,128)(2,1)}, u32[]{:S(2)}) %copy-start.1) | copy-done | bytes 524312
  72.5 0.0 copy-start.2
  72.5 0.7 copy-done.2
  73.2 1.2 %shard_map.59 = (f32[1,1024]{1,0:T(1,128)}, bf16[1024,256]{1,0:T(8,128)(2,1)}, bf16[2048,256]{1,0:T(8,128)(2,1)}) custom-call(f32[1,1024]{1,0:T(1,128)S(1)} %copy-done.2, bf16[1024,256]{1,0:T(8,128)(2,1)S(1)} %copy-done.1, bf16[2048,256]{1,0:T(8,128)(2,1)S(1)} %copy-done), custom_call_target="tpu_custom_call" | custom-call | tf_op jit(solution)/shard_map/pallas_call | solution.py:309
Async XLA Ops:
  70.2 1.2 %copy-start = (bf16[2048,256]{1,0:T(8,128)(2,1)S(1)}, bf16[2048,256]{1,0:T(8,128)(2,1)}, u32[]{:S(2)}) copy-start(bf16[2048,256]{1,0:T(8,128)(2,1)} %get-tuple-element.11.c) | copy-start | bytes 3145732
  71.5 1.0 %copy-start.1 = (bf16[1024,256]{1,0:T(8,128)(2,1)S(1)}, bf16[1024,256]{1,0:T(8,128)(2,1)}, u32[]{:S(2)}) copy-start(bf16[1024,256]{1,0:T(8,128)(2,1)} %get-tuple-element.10.b) | copy-start | bytes 1572868
  72.5 0.7 copy-start.2
